TPU v7x, 256 devices: a whole 4x4x8 slice. The times are simulated.
256 devices in a mesh: row: 16 (over x_hi, y, core), col: 16 (over z, x_lo).
Axes of the slice: x: 4 (x_hi: 2, x_lo: 2; x = x_hi * 2 + x_lo), y: 4, z: 8, core: 2. Of those that a mesh axis runs over, the one named last changes fastest.
Arguments:
- out_grad: bfloat16 [2048, 8192], P('row', 'col'), may hold values from -6 to 6
- acts: bfloat16 [2048, 28672], P('col', 'row'), may hold values from -4 to 4
- weight: bfloat16 [28672, 8192], P('row', 'col'), may hold values from -0.03125 to 0.03125
Outputs:
- input_grad: bfloat16 [2048, 28672], P('col', 'row')
- weight_grad: float32 [28672, 8192], P('row', 'col')
All inputs are finite; a program needn't handle non-finite values.
Results may differ from a plain program's by a relative error of at most 0.001.
Values may be sent and summed in bfloat16 or wider, within the bound.
A program may use at most 128 MiB of HBM per device.

v0:
```python
import math

import jax
import jax.numpy as jnp
from jax import lax
from jax.sharding import PartitionSpec as P


def body(out_grad, acts, weight):
    tok_rows = lax.all_gather(out_grad, "row", axis=0, tiled=True)
    tokens_all = tok_rows.shape[0]
    input_sum = lax.psum_scatter(
        lax.dot_general(
            tok_rows, weight, (((1,), (1,)), ((), ())), preferred_element_type=jnp.float32
        ),
        "col",
        scatter_dimension=0,
        tiled=True,
    )
    input_grad = input_sum.astype(jnp.bfloat16)
    summed = lax.dot_general(
        lax.all_gather(acts, "col", axis=0, tiled=True),
        tok_rows,
        (((0,), (0,)), ((), ())),
        preferred_element_type=jnp.float32,
    )
    weight_grad = summed * (1.0 / math.sqrt(tokens_all))
    return (input_grad, weight_grad)


def solution(mesh):
    in_specs = (P("row", "col"), P("col", "row"), P("row", "col"))
    out_specs = (P("col", "row"), P("row", "col"))
    return jax.shard_map(body, mesh=mesh, in_specs=in_specs, out_specs=out_specs, check_vma=False)
```

profile of v0, /device:TPU:8, one launch (start us, length us, event | category | flops | bytes accessed | tf_op | source)
XLA Modules:
  0.0 549.7 jit_solution(11433787250721069641)
XLA Ops:
  7.2 0.0 copy-start
  7.2 0.0 all-gather.3.cloned.1.call-start
  7.2 0.7 all-gather.3.cloned.1.call-update
  7.9 0.0 all-gather.5.cloned.1.call-start
  8.0 0.7 all-gather.5.cloned.1.call-update
  8.7 0.0 reduce-scatter.2.cloned.1.call-start
  8.7 57.3 %all-gather.3.cloned.1.call-done = bf16[2048,512]{1,0:T(8,128)(2,1)} async-done(((bf16[128,512]{1,0:T(8,128)(2,1)}), bf16[2048,512]{1,0:T(8,128)(2,1)}) %all-gather.3.cloned.1.call-update) | async-done | bytes 2097168 | tf_op jit(solution)/shard_map/all_gather | solution.py:10
  66.0 0.0 copy-done
  66.0 9.3 %fusion = f32[2048,1792]{1,0:T(8,128)} fusion(bf16[2048,512]{1,0:T(8,128)(2,1)} %all-gather.3.cloned.1.call-done, bf16[1792,512]{1,0:T(8,128)(2,1)S(1)} %copy-done), kind=kOutput, calls=%fused_computation.1 | convolution fusion | flops 3758096384 | bytes 18612224 | tf_op jit(solution)/shard_map/dot_general | solution.py:13
  75.3 0.0 reduce-scatter.2.cloned.1.call-update
  75.3 153.4 %all-gather.5.cloned.1.call-done = bf16[2048,1792]{1,0:T(8,128)(2,1)} async-done(((bf16[128,1792]{1,0:T(8,128)(2,1)}), bf16[2048,1792]{1,0:T(8,128)(2,1)}) %all-gather.5.cloned.1.call-update) | async-done | bytes 7340048 | tf_op jit(solution)/shard_map/all_gather | solution.py:22
  228.7 9.5 %convolution_multiply_fusion = f32[1792,512]{1,0:T(8,128)} fusion(bf16[2048,1792]{1,0:T(8,128)(2,1)} %all-gather.5.cloned.1.call-done, bf16[2048,512]{1,0:T(8,128)(2,1)} %all-gather.3.cloned.1.call-done), kind=kOutput, calls=%fused_computation | convolution fusion | flops 3759013888 | bytes 13107200 | tf_op jit(solution)/shard_map/dot_general | solution.py:21
  238.2 302.9 %reduce-scatter.2.cloned.1.call-done = f32[128,1792]{1,0:T(8,128)} async-done(((f32[2048,1792]{1,0:T(8,128)}), f32[128,1792]{1,0:T(8,128)}) %reduce-scatter.2.cloned.1.call-update) | async-done | bytes 917520 | tf_op jit(solution)/shard_map/reduce_scatter | solution.py:12
  541.1 2.0 convert_element_type.3
Async XLA Ops:
  7.2 58.8 %copy-start = (bf16[1792,512]{1,0:T(8,128)(2,1)S(1)}, bf16[1792,512]{1,0:T(8,128)(2,1)}, u32[]{:S(2)}) copy-start(bf16[1792,512]{1,0:T(8,128)(2,1)} %param.5) | copy-start | bytes 5505028
  7.2 58.8 %all-gather.3.cloned.1.call-start = ((), (), s32[]{:S(2)}) async-start(), calls=%async_computation.1 | async-start | bytes 2228224 | tf_op jit(solution)/shard_map/all_gather | solution.py:10
  7.9 220.8 %all-gather.5.cloned.1.call-start = ((), (), s32[]{:S(2)}) async-start(), calls=%async_computation.3 | async-start | bytes 7798784 | tf_op jit(solution)/shard_map/all_gather | solution.py:22
  8.7 532.5 %reduce-scatter.2.cloned.1.call-start = ((), (), s32[]{:S(2)}) async-start(), calls=%async_computation.2 | async-start | bytes 15597568 | tf_op jit(solution)/shard_map/reduce_scatter | solution.py:12
Sparse Core Ops, SparseCore 0:
  10.8 55.1 all-gather.2
  67.7 160.9 all-gather.4
  231.3 309.8 reduce-scatter.1
where the time goes:
time: 551 us; the launch traced here: 550 us
  waiting for transfers between devices  515 us (93%)
  matrix products  18.8 us (3%)
  between operations  13.8 us (3%)
    reduce_scatter x1, waiting for transfers between devices, body(): lax.psum_scatter(lax.dot_general(tok_rows, weight, (((1,), (1,)), ((), ()...  303 us
    all_gather x1, waiting for transfers between devices, body(): lax.all_gather(acts, 'col', axis=0, tiled=True)  153 us
    all_gather x1, waiting for transfers between devices, body(): tok_rows = lax.all_gather(out_grad, 'row', axis=0, tiled=True)  57.3 us
  transfers between devices with their start and end apart: 3, of which 3 were waited for; matrix products, arithmetic and copies ran while one was open for 3% of the time, Pallas kernels for 0%

commit v1 on v0

v1 whole, which is shorter than its diff:
```python
import functools
import math

import jax
import jax.numpy as jnp
from jax import lax
from jax.experimental import pallas as pl
from jax.experimental.pallas import tpu as pltpu
from jax.sharding import PartitionSpec as P

MESH = pl.DeviceIdType.MESH
F32, BF16 = jnp.float32, jnp.bfloat16
NZ, NY = 8, 4
TOK = 128
NJ, FC = 7, 256
TOP = 87.0


def encode(parts, out_ref, rows):
    most = functools.reduce(jnp.maximum, [jnp.max(jnp.abs(p), axis=0, keepdims=True) for p in parts])
    scale = jnp.maximum(most * 1.01, 1e-35).astype(BF16)
    gain = (2 * TOP) / scale.astype(F32)
    for i, p in enumerate(parts):
        code = jnp.exp(jnp.abs(p) * gain - TOP)
        out_ref[pl.ds(i * rows, rows), :] = jnp.where(p < 0, -code, code).astype(BF16)
    out_ref[pl.ds(len(parts) * rows, 16), :] = jnp.broadcast_to(scale, (16, 128))


def decode(in_ref, count, rows):
    scale = in_ref[pl.ds(count * rows, 16), :].astype(F32)[:1] * (1.0 / (2 * TOP))
    parts = []
    for i in range(count):
        code = in_ref[pl.ds(i * rows, rows), :].astype(F32)
        value = (jnp.log(jnp.abs(code)) + TOP) * scale
        parts.append(jnp.where(code < 0, -value, value))
    return parts


def kernel(
    lag, scaling, g_ref, a_ref, w_ref, ig_ref, wg_ref,
    gbuf, wx, abuf, pbuf, own, h_snd, h_rcv, f_snd, f_rcv, x_snd, x_rcv,
    gx_s, gx_r, gy_s, gy_r, gs_s, gs_r, w_s, w_r, a_s, a_r, r_s, r_r, x_s, x_r, o_s,
):
    row, col = lax.axis_index("row"), lax.axis_index("col")
    xh, y, core = row // (2 * NY), (row // 2) % NY, row % 2
    z, xl = col // 2, col % 2
    hub = core == xl

    def dev(xh=xh, y=y, core=core, z=z, xl=xl):
        return {"row": (xh * NY + y) * 2 + core, "col": z * 2 + xl}

    def copy(src, dst, s_sem, r_sem, to):
        return pltpu.make_async_remote_copy(
            src_ref=src, dst_ref=dst, send_sem=s_sem, recv_sem=r_sem, device_id=to, device_id_type=MESH
        )

    ring = (dev(z=(z + 1) % NZ), dev(z=(z + NZ - 1) % NZ))
    across = dev(xl=1 - xl)
    sibling = dev(core=1 - core)
    y_peers = [dev(y=(y + d) % NY) for d in (1, 2, 3)]

    for j in range(NJ):
        abuf[j, pl.ds(z * TOK, TOK), :] = a_ref[:, j * FC : (j + 1) * FC]

    peers = [*ring, across, dev(xh=1 - xh), dev(xh=1 - xh, xl=1 - xl), sibling, *y_peers]
    barrier = pltpu.get_barrier_semaphore()
    for peer in peers:
        pl.semaphore_signal(barrier, inc=1, device_id=peer, device_id_type=MESH)
    pl.semaphore_wait(barrier, len(peers))

    def a_copy(d, s, j, arriving=False):
        back = s + 1 if arriving else s
        origin = (z + NZ - back) % NZ if d == 0 else (z + back) % NZ
        start, size = (origin * TOK + d * (TOK // 2), TOK // 2) if s == 3 else (origin * TOK, TOK)
        block = abuf.at[j, pl.ds(start, size)]
        return copy(block, block, a_s.at[d, s, j], a_r.at[d, s, j], ring[d])

    def forward(s):
        @pl.loop(0, NJ)
        def _(j):
            for d in range(2):
                if s > 0:
                    a_copy(d, s - 1, j, True).wait_recv()
                a_copy(d, s, j).start()

    forward(0)

    def g_block(xh_, y_, xl_):
        return gbuf.at[xl_, pl.ds((xh_ * NY + y_) * TOK, TOK)]

    def gx_copy(to_xh, n, src_xh, src_xl):
        block = g_block(src_xh, y, src_xl)
        return copy(g_ref, block, gx_s.at[n], gx_r.at[src_xl * 2 + src_xh], dev(xh=to_xh, xl=core))

    @pl.when(hub)
    def _():
        gx_copy(1 - xh, 0, xh, xl).start()
        gbuf[xl, pl.ds((xh * NY + y) * TOK, TOK), :] = g_ref[...]

    @pl.when(jnp.logical_not(hub))
    def _():
        gx_copy(xh, 0, xh, xl).start()
        gx_copy(1 - xh, 1, xh, xl).start()

    def w_copy(j):
        rows = pl.ds(j * FC, FC)
        return copy(w_ref.at[rows], wx.at[rows], w_s.at[j], w_r.at[j], across)

    @pl.loop(0, NJ)
    def _(j):
        w_copy(j).start()

    def gy_copy(b, n, arriving=False):
        y_ = (y + NY - (n + 1)) % NY if arriving else y
        block = g_block(b % 2, y_, b // 2)
        return copy(block, block, gy_s.at[n, b], gy_r.at[n, b], y_peers[n])

    def gs_copy(b, n):
        block = g_block(b % 2, (y + NY - n) % NY, b // 2)
        return copy(block, block, gs_s.at[n, b], gs_r.at[n, b], sibling)

    @pl.when(hub)
    def _():
        for src_xh, src_xl in ((xh, 1 - xl), (1 - xh, 1 - xl), (1 - xh, xl)):
            gx_copy(xh, 0, src_xh, src_xl).wait_recv()

        @pl.loop(0, 4)
        def _(b):
            for n in (0, 2, 1):
                gy_copy(b, n).start()
            gs_copy(b, 0).start()

    forward(1)

    @pl.when(hub)
    def _():
        for n in (0, 2, 1):

            @pl.loop(0, 4)
            def _(b):
                gy_copy(b, n, True).wait_recv()
                gs_copy(b, n + 1).start()

    forward(2)

    @pl.when(jnp.logical_not(hub))
    def _():
        for n in (0, 1, 3, 2):

            @pl.loop(0, 4)
            def _(b):
                gs_copy(b, n).wait_recv()

    forward(3)

    def rs_copy(d, s, j):
        if s == 0:
            return copy(h_snd.at[d, j], h_rcv.at[d, j], r_s.at[d, s, j], r_r.at[d, s, j], ring[d])
        return copy(f_snd.at[d, s - 1, j], f_rcv.at[d, s - 1, j], r_s.at[d, s, j], r_r.at[d, s, j], ring[d])

    def halves(j, owner):
        rows = pl.ds(owner * TOK, TOK)
        return [pbuf[j, rows, :128], pbuf[j, rows, 128:]]

    def partial(j):
        w_copy(j).wait_recv()
        rows = pl.ds(j * FC, FC)
        nt = (((1,), (1,)), ((), ()))
        pbuf[j] = lax.dot_general(gbuf[xl], w_ref[rows], nt, preferred_element_type=F32) + lax.dot_general(
            gbuf[1 - xl], wx[rows], nt, preferred_element_type=F32
        )
        far = halves(j, (z + 4) % NZ)
        for d in range(2):
            encode([far[d]], h_snd.at[d, j], TOK)
            rs_copy(d, 0, j).start()

    def pass_on(s, j):
        for d in range(2):
            rs_copy(d, s - 1, j).wait_recv()
            owner = (z + 4 - s) % NZ if d == 0 else (z + 4 + s) % NZ
            parts = halves(j, owner)
            if s == 1:
                (arrived,) = decode(h_rcv.at[d, j], 1, TOK)
                parts[d] = parts[d] + arrived
            else:
                arrived = decode(f_rcv.at[d, s - 2, j], 2, TOK)
                parts = [p + q for p, q in zip(parts, arrived)]
            encode(parts, f_snd.at[d, s - 1, j], TOK)
            rs_copy(d, s, j).start()

    def finish(j):
        parts = halves(j, z)
        for d in range(2):
            rs_copy(d, 3, j).wait_recv()
            parts = [p + q for p, q in zip(parts, decode(f_rcv.at[d, 2, j], 2, TOK))]
        for i in range(2):
            ig_ref[:, pl.ds(pl.multiple_of(j * FC + i * 128, 128), 128)] = parts[i].astype(BF16)

    def x_copy(j):
        return copy(x_snd.at[j], x_rcv.at[j], x_s.at[j], x_r.at[j], across)

    def weight_part(j):
        for d in range(2):
            a_copy(d, 3, j, True).wait_recv()
        tn = (((0,), (0,)), ((), ()))
        theirs = scaling * lax.dot_general(abuf[j], gbuf[1 - xl], tn, preferred_element_type=F32)
        encode([theirs[:, i * 128 : (i + 1) * 128] for i in range(4)], x_snd.at[j], FC)
        x_copy(j).start()
        own[j] = scaling * lax.dot_general(abuf[j], gbuf[xl], tn, preferred_element_type=F32)

    def out_copy(j):
        return pltpu.make_async_copy(own.at[j], wg_ref.at[pl.ds(j * FC, FC)], o_s.at[j])

    @pl.loop(0, NJ + 4 * lag)
    def _(i):
        def at(delay, work):
            @pl.when(jnp.logical_and(i >= delay, i < NJ + delay))
            def _():
                work(i - delay)

        at(0, partial)
        at(lag, functools.partial(pass_on, 1))
        at(0, weight_part)
        at(2 * lag, functools.partial(pass_on, 2))
        at(3 * lag, functools.partial(pass_on, 3))
        at(4 * lag, finish)

    @pl.loop(0, NJ)
    def _(j):
        x_copy(j).wait_recv()
        arrived = decode(x_rcv.at[j], 4, FC)
        for i in range(4):
            lanes = slice(i * 128, (i + 1) * 128)
            own[j, :, lanes] = own[j, :, lanes] + arrived[i]
        out_copy(j).start()

    @pl.loop(0, NJ)
    def _(j):
        w_copy(j).wait_send()
        x_copy(j).wait_send()
        for d in range(2):
            for s in range(4):
                a_copy(d, s, j).wait_send()
                rs_copy(d, s, j).wait_send()
        out_copy(j).wait()

    @pl.when(hub)
    def _():
        gx_copy(1 - xh, 0, xh, xl).wait_send()

        @pl.loop(0, 4)
        def _(b):
            for n in range(3):
                gy_copy(b, n).wait_send()
            for n in range(4):
                gs_copy(b, n).wait_send()

    @pl.when(jnp.logical_not(hub))
    def _():
        gx_copy(xh, 0, xh, xl).wait_send()
        gx_copy(1 - xh, 1, xh, xl).wait_send()


def body(out_grad, acts, weight):
    dma = pltpu.SemaphoreType.DMA
    ff, features = weight.shape
    return pl.pallas_call(
        functools.partial(kernel, 1, 1.0 / math.sqrt(TOK * 16)),
        out_shape=(jax.ShapeDtypeStruct(acts.shape, BF16), jax.ShapeDtypeStruct(weight.shape, F32)),
        in_specs=[pl.BlockSpec(memory_space=pltpu.VMEM)] * 3,
        out_specs=(pl.BlockSpec(memory_space=pltpu.VMEM), pl.BlockSpec(memory_space=pl.ANY)),
        scratch_shapes=[
            pltpu.VMEM((2, NZ * TOK, features), BF16),
            pltpu.VMEM((ff, features), BF16),
            pltpu.VMEM((NJ, NZ * TOK, FC), BF16),
            pltpu.VMEM((NJ, NZ * TOK, FC), F32),
            pltpu.VMEM((NJ, FC, features), F32),
            pltpu.VMEM((2, NJ, TOK + 16, 128), BF16),
            pltpu.VMEM((2, NJ, TOK + 16, 128), BF16),
            pltpu.VMEM((2, 3, NJ, 2 * TOK + 16, 128), BF16),
            pltpu.VMEM((2, 3, NJ, 2 * TOK + 16, 128), BF16),
            pltpu.VMEM((NJ, 4 * FC + 16, 128), BF16),
            pltpu.VMEM((NJ, 4 * FC + 16, 128), BF16),
            dma((2,)), dma((4,)),
            dma((3, 4)), dma((3, 4)),
            dma((4, 4)), dma((4, 4)),
            dma((NJ,)), dma((NJ,)),
            dma((2, 4, NJ)), dma((2, 4, NJ)),
            dma((2, 4, NJ)), dma((2, 4, NJ)),
            dma((NJ,)), dma((NJ,)),
            dma((NJ,)),
        ],
        compiler_params=pltpu.CompilerParams(
            collective_id=0, has_side_effects=True, vmem_limit_bytes=58 * 2**20
        ),
        cost_estimate=pl.CostEstimate(
            flops=8 * NZ * TOK * ff * features, bytes_accessed=16 * 2**20, transcendentals=6 * 2**20
        ),
    )(out_grad, acts, weight)


def solution(mesh):
    in_specs = (P("row", "col"), P("col", "row"), P("row", "col"))
    out_specs = (P("col", "row"), P("row", "col"))
    return jax.shard_map(body, mesh=mesh, in_specs=in_specs, out_specs=out_specs, check_vma=False)
```

time: 551 us -> 103 us (0.19)
  waiting for transfers between devices: 515 us -> 0 us
  Pallas kernels: 0 us -> 96.5 us
  matrix products: 18.8 us -> 0 us
  between operations: 13.8 us -> 0.64 us
  local copies, waits for them, and re-layouts: 0.01 us -> 6.06 us
    reduce_scatter x1 -> x0, waiting for transfers between devices: 303 us -> none  [body(): lax.psum_scatter(lax.dot_general(tok_rows, weight, (((1,), (1,)), ((), ()...]
    all_gather x2 -> x0, waiting for transfers between devices: 211 us -> none  [the longest x1 153 us: body(): lax.all_gather(acts, 'col', axis=0, tiled=True)]
    pallas_call x0 -> x1, Pallas kernels: none -> 96.5 us  [body(): pl.pallas_call(functools.partial(kernel, 1, 1.0 / math.sqrt(TOK * 16)), o...]
    dot_general x2 -> x0, matrix products: 18.8 us -> none  [the longest x1 9.52 us: body(): lax.dot_general(lax.all_gather(acts, 'col', axis=0, tiled=True), tok_rows...]
    unnamed x2, local copies, waits for them, and re-layouts: 0.01 us -> 6.06 us
  transfers between devices with their start and end apart: 3 -> 0, of which waited for: 3 -> 0; matrix products, arithmetic and copies ran while one was open for 3% -> 0% of each run, Pallas kernels for 0% -> 0%
where the time goes in v1:
time: 103 us
  Pallas kernels  96.5 us (94%)
  local copies, waits for them, and re-layouts  6.06 us (6%)
    pallas_call x1, Pallas kernels, body(): pl.pallas_call(functools.partial(kernel, 1, 1.0 / math.sqrt(TOK * 16)), o...  96.5 us
    unnamed x2, local copies, waits for them, and re-layouts  6.06 us

profile of v1, /device:TPU:8, one launch (start us, length us, event | category | flops | bytes accessed | tf_op | source)
XLA Modules:
  0.0 103.2 jit_solution(5610168386105099893)
XLA Ops:
  0.6 96.5 %shard_map.50 = (bf16[128,1792]{1,0:T(8,128)(2,1)}, f32[1792,512]{1,0:T(8,128)}) custom-call(bf16[128,512]{1,0:T(8,128)(2,1)} %g_ref.1, bf16[128,1792]{1,0:T(8,128)(2,1)} %a_ref.1, bf16[1792,512]{1,0:T(8,128)(2,1)} %w_ref.1), custom_call_target="tpu_custom_call" | custom-call | flops 7516192768 | bytes 16777216 | tf_op jit(solution)/shard_map/pallas_call | solution.py:267
  97.1 1.8 %copy.7 = bf16[128,1792]{1,0:T(8,128)(2,1)} copy(bf16[128,1792]{1,0:T(8,128)(2,1)} %get-tuple-element.4) | data formatting | bytes 917504
  98.9 4.2 %copy.8 = f32[1792,512]{1,0:T(8,128)} copy(f32[1792,512]{1,0:T(8,128)} %get-tuple-element.5) | data formatting | bytes 7340032

commit v2 on v1

--- a/solution.py
+++ b/solution.py
@@ -38,8 +38,8 @@
 
 def kernel(
     lag, scaling, g_ref, a_ref, w_ref, ig_ref, wg_ref,
-    gbuf, wx, abuf, pbuf, own, h_snd, h_rcv, f_snd, f_rcv, x_snd, x_rcv,
-    gx_s, gx_r, gy_s, gy_r, gs_s, gs_r, w_s, w_r, a_s, a_r, r_s, r_r, x_s, x_r, o_s,
+    gbuf, wx, w_here, abuf, pbuf, h_snd, h_rcv, f_snd, f_rcv, x_snd, x_rcv,
+    gx_s, gx_r, gy_s, gy_r, gs_s, gs_r, w_s, w_r, a_s, a_r, r_s, r_r, x_s, x_r, l_s,
 ):
     row, col = lax.axis_index("row"), lax.axis_index("col")
     xh, y, core = row // (2 * NY), (row // 2) % NY, row % 2
@@ -59,8 +59,20 @@
     sibling = dev(core=1 - core)
     y_peers = [dev(y=(y + d) % NY) for d in (1, 2, 3)]
 
+    def a_load(j):
+        lanes = pl.ds(pl.multiple_of(j * FC, FC), FC)
+        return pltpu.make_async_copy(a_ref.at[:, lanes], abuf.at[j, pl.ds(z * TOK, TOK)], l_s.at[j])
+
+    w_load = pltpu.make_async_copy(w_ref, w_here, l_s.at[NJ])
+    g_load = pltpu.make_async_copy(g_ref, gbuf.at[xl, pl.ds((xh * NY + y) * TOK, TOK)], l_s.at[NJ + 1])
     for j in range(NJ):
-        abuf[j, pl.ds(z * TOK, TOK), :] = a_ref[:, j * FC : (j + 1) * FC]
+        a_load(j).start()
+
+    @pl.when(hub)
+    def _():
+        g_load.start()
+
+    w_load.start()
 
     peers = [*ring, across, dev(xh=1 - xh), dev(xh=1 - xh, xl=1 - xl), sibling, *y_peers]
     barrier = pltpu.get_barrier_semaphore()
@@ -81,9 +93,9 @@
             for d in range(2):
                 if s > 0:
                     a_copy(d, s - 1, j, True).wait_recv()
+                elif d == 0:
+                    a_load(j).wait()
                 a_copy(d, s, j).start()
-
-    forward(0)
 
     def g_block(xh_, y_, xl_):
         return gbuf.at[xl_, pl.ds((xh_ * NY + y_) * TOK, TOK)]
@@ -95,7 +107,7 @@
     @pl.when(hub)
     def _():
         gx_copy(1 - xh, 0, xh, xl).start()
-        gbuf[xl, pl.ds((xh * NY + y) * TOK, TOK), :] = g_ref[...]
+        g_load.wait()
 
     @pl.when(jnp.logical_not(hub))
     def _():
@@ -109,6 +121,8 @@
     @pl.loop(0, NJ)
     def _(j):
         w_copy(j).start()
+
+    forward(0)
 
     def gy_copy(b, n, arriving=False):
         y_ = (y + NY - (n + 1)) % NY if arriving else y
@@ -152,6 +166,7 @@
                 gs_copy(b, n).wait_recv()
 
     forward(3)
+    w_load.wait()
 
     def rs_copy(d, s, j):
         if s == 0:
@@ -166,7 +181,7 @@
         w_copy(j).wait_recv()
         rows = pl.ds(j * FC, FC)
         nt = (((1,), (1,)), ((), ()))
-        pbuf[j] = lax.dot_general(gbuf[xl], w_ref[rows], nt, preferred_element_type=F32) + lax.dot_general(
+        pbuf[j] = lax.dot_general(gbuf[xl], w_here[rows], nt, preferred_element_type=F32) + lax.dot_general(
             gbuf[1 - xl], wx[rows], nt, preferred_element_type=F32
         )
         far = halves(j, (z + 4) % NZ)
@@ -206,10 +221,7 @@
         theirs = scaling * lax.dot_general(abuf[j], gbuf[1 - xl], tn, preferred_element_type=F32)
         encode([theirs[:, i * 128 : (i + 1) * 128] for i in range(4)], x_snd.at[j], FC)
         x_copy(j).start()
-        own[j] = scaling * lax.dot_general(abuf[j], gbuf[xl], tn, preferred_element_type=F32)
-
-    def out_copy(j):
-        return pltpu.make_async_copy(own.at[j], wg_ref.at[pl.ds(j * FC, FC)], o_s.at[j])
+        wg_ref[pl.ds(j * FC, FC), :] = scaling * lax.dot_general(abuf[j], gbuf[xl], tn, preferred_element_type=F32)
 
     @pl.loop(0, NJ + 4 * lag)
     def _(i):
@@ -231,8 +243,8 @@
         arrived = decode(x_rcv.at[j], 4, FC)
         for i in range(4):
             lanes = slice(i * 128, (i + 1) * 128)
-            own[j, :, lanes] = own[j, :, lanes] + arrived[i]
-        out_copy(j).start()
+            rows = pl.ds(j * FC, FC)
+            wg_ref[rows, lanes] = wg_ref[rows, lanes] + arrived[i]
 
     @pl.loop(0, NJ)
     def _(j):
@@ -242,7 +254,6 @@
             for s in range(4):
                 a_copy(d, s, j).wait_send()
                 rs_copy(d, s, j).wait_send()
-        out_copy(j).wait()
 
     @pl.when(hub)
     def _():
@@ -266,15 +277,15 @@
     ff, features = weight.shape
     return pl.pallas_call(
         functools.partial(kernel, 1, 1.0 / math.sqrt(TOK * 16)),
-        out_shape=(jax.ShapeDtypeStruct(acts.shape, BF16), jax.ShapeDtypeStruct(weight.shape, F32)),
-        in_specs=[pl.BlockSpec(memory_space=pltpu.VMEM)] * 3,
-        out_specs=(pl.BlockSpec(memory_space=pltpu.VMEM), pl.BlockSpec(memory_space=pl.ANY)),
+        out_shape=(pltpu.VMEM(acts.shape, BF16), pltpu.VMEM(weight.shape, F32)),
+        in_specs=[pl.BlockSpec(memory_space=pltpu.HBM)] * 3,
+        out_specs=(pl.BlockSpec(memory_space=pltpu.VMEM), pl.BlockSpec(memory_space=pltpu.VMEM)),
         scratch_shapes=[
             pltpu.VMEM((2, NZ * TOK, features), BF16),
             pltpu.VMEM((ff, features), BF16),
+            pltpu.VMEM((ff, features), BF16),
             pltpu.VMEM((NJ, NZ * TOK, FC), BF16),
             pltpu.VMEM((NJ, NZ * TOK, FC), F32),
-            pltpu.VMEM((NJ, FC, features), F32),
             pltpu.VMEM((2, NJ, TOK + 16, 128), BF16),
             pltpu.VMEM((2, NJ, TOK + 16, 128), BF16),
             pltpu.VMEM((2, 3, NJ, 2 * TOK + 16, 128), BF16),
@@ -288,10 +299,10 @@
             dma((2, 4, NJ)), dma((2, 4, NJ)),
             dma((2, 4, NJ)), dma((2, 4, NJ)),
             dma((NJ,)), dma((NJ,)),
-            dma((NJ,)),
+            dma((NJ + 2,)),
         ],
         compiler_params=pltpu.CompilerParams(
-            collective_id=0, has_side_effects=True, vmem_limit_bytes=58 * 2**20
+            collective_id=0, has_side_effects=True, vmem_limit_bytes=56 * 2**20
         ),
         cost_estimate=pl.CostEstimate(
             flops=8 * NZ * TOK * ff * features, bytes_accessed=16 * 2**20, transcendentals=6 * 2**20

time: 103 us -> 96.9 us (0.941)
  local copies, waits for them, and re-layouts: 6.06 us -> 2.61 us
  Pallas kernels: 96.5 us -> 93.6 us
    unnamed x2, local copies, waits for them, and re-layouts: 6.06 us -> 2.61 us
    pallas_call x1, Pallas kernels: 96.5 us -> 93.6 us  [body(): pl.pallas_call(functools.partial(kernel, 1, 1.0 / math.sqrt(TOK * 16)), o...]
where the time goes in v2:
time: 96.9 us; the launch traced here: 96.8 us
  Pallas kernels  93.6 us (97%)
  local copies, waits for them, and re-layouts  2.61 us (3%)
    pallas_call x1, Pallas kernels, body(): pl.pallas_call(functools.partial(kernel, 1, 1.0 / math.sqrt(TOK * 16)), o...  93.6 us
    unnamed x2, local copies, waits for them, and re-layouts  2.61 us

profile of v2, /device:TPU:8, one launch (start us, length us, event | category | flops | bytes accessed | tf_op | source)
XLA Modules:
  0.0 96.8 jit_solution(6155114588470272148)
XLA Ops:
  0.6 93.6 %shard_map.50 = (bf16[128,1792]{1,0:T(8,128)(2,1)S(1)}, f32[1792,512]{1,0:T(8,128)S(1)}) custom-call(bf16[128,512]{1,0:T(8,128)(2,1)} %g_ref.1, bf16[128,1792]{1,0:T(8,128)(2,1)} %a_ref.1, bf16[1792,512]{1,0:T(8,128)(2,1)} %w_ref.1), custom_call_target="tpu_custom_call" | custom-call | flops 7516192768 | bytes 16777216 | tf_op jit(solution)/shard_map/pallas_call | solution.py:278
  94.2 0.8 copy.7
  95.0 1.8 %copy.8 = f32[1792,512]{1,0:T(8,128)} copy(f32[1792,512]{1,0:T(8,128)S(1)} %get-tuple-element.3) | data formatting | bytes 7340032

commit v3 on v2

v3 whole, which is shorter than its diff:
```python
import functools
import math

import jax
import jax.numpy as jnp
from jax import lax
from jax.experimental import pallas as pl
from jax.experimental.pallas import tpu as pltpu
from jax.sharding import PartitionSpec as P

MESH = pl.DeviceIdType.MESH
F32, BF16 = jnp.float32, jnp.bfloat16
NZ, NY = 8, 4
TOK = 128
NJ, FC = 7, 256
HC = FC // 2
TOP = 87.0


def encode(parts, out_ref, rows):
    most = functools.reduce(jnp.maximum, [jnp.max(jnp.abs(p), axis=0, keepdims=True) for p in parts])
    scale = jnp.maximum(most * 1.01, 1e-35).astype(BF16)
    gain = (2 * TOP) / scale.astype(F32)
    for i, p in enumerate(parts):
        code = jnp.exp(jnp.abs(p) * gain - TOP)
        out_ref[pl.ds(i * rows, rows), :] = jnp.where(p < 0, -code, code).astype(BF16)
    out_ref[pl.ds(len(parts) * rows, 16), :] = jnp.broadcast_to(scale, (16, 128))


def decode(in_ref, count, rows):
    scale = in_ref[pl.ds(count * rows, 16), :].astype(F32)[:1] * (1.0 / (2 * TOP))
    parts = []
    for i in range(count):
        code = in_ref[pl.ds(i * rows, rows), :].astype(F32)
        value = (jnp.log(jnp.abs(code)) + TOP) * scale
        parts.append(jnp.where(code < 0, -value, value))
    return parts


def kernel(
    lag, scaling, g_ref, a_ref, w_ref, ig_ref, wg_ref,
    gbuf, wx, w_here, abuf, pbuf, h_snd, h_rcv, f_snd, f_rcv, x_snd, x_rcv, i_snd, i_rcv,
    gx_s, gx_r, gy_s, gy_r, gf_s, gf_r, gs_s, gs_r, w_s, w_r, a_s, a_r, r_s, r_r, x_s, x_r, i_s, i_r, l_s,
):
    row, col = lax.axis_index("row"), lax.axis_index("col")
    xh, y, core = row // (2 * NY), (row // 2) % NY, row % 2
    z, xl = col // 2, col % 2
    half = NJ * HC

    def dev(xh=xh, y=y, core=core, z=z, xl=xl):
        return {"row": (xh * NY + y) * 2 + core, "col": z * 2 + xl}

    def copy(src, dst, s_sem, r_sem, to):
        return pltpu.make_async_remote_copy(
            src_ref=src, dst_ref=dst, send_sem=s_sem, recv_sem=r_sem, device_id=to, device_id_type=MESH
        )

    ring = (dev(z=(z + 1) % NZ), dev(z=(z + NZ - 1) % NZ))
    across = dev(xl=1 - xl)
    sibling = dev(core=1 - core)
    y_peers = [dev(y=(y + d) % NY) for d in (1, 3, 2)]
    x_peers = [dev(xl=1 - xl), dev(xh=1 - xh, xl=1 - xl), dev(xh=1 - xh)]

    def a_load(j):
        lanes = pl.ds(pl.multiple_of(j * FC, FC), FC)
        return pltpu.make_async_copy(a_ref.at[:, lanes], abuf.at[j, pl.ds(z * TOK, TOK)], l_s.at[j])

    w_load = pltpu.make_async_copy(w_ref, w_here, l_s.at[NJ])
    g_load = pltpu.make_async_copy(
        g_ref, gbuf.at[xl, pl.ds(((core * 2 + xh) * NY + y) * TOK, TOK)], l_s.at[NJ + 1]
    )
    for j in range(NJ):
        a_load(j).start()

    g_load.start()
    w_load.start()

    peers = [*ring, *x_peers, sibling, *y_peers]
    barrier = pltpu.get_barrier_semaphore()
    for peer in peers:
        pl.semaphore_signal(barrier, inc=1, device_id=peer, device_id_type=MESH)
    pl.semaphore_wait(barrier, len(peers))

    def a_copy(d, s, j, arriving=False):
        back = s + 1 if arriving else s
        origin = (z + NZ - back) % NZ if d == 0 else (z + back) % NZ
        start, size = (origin * TOK + d * (TOK // 2), TOK // 2) if s == 3 else (origin * TOK, TOK)
        block = abuf.at[j, pl.ds(start, size)]
        return copy(block, block, a_s.at[d, s, j], a_r.at[d, s, j], ring[d])

    def a_step(s, j):
        if s == 0:
            a_load(j).wait()
        for d in range(2):
            if s > 0:
                a_copy(d, s - 1, j, True).wait_recv()
            a_copy(d, s, j).start()

    def slot(t):
        for s in range(4):
            if 0 <= t - s < NJ:
                a_step(s, t - s)

    def g_block(xh_, y_, xl_, core_):
        return gbuf.at[xl_, pl.ds(((core_ * 2 + xh_) * NY + y_) * TOK, TOK)]

    sources = [(xh, xl), (xh, 1 - xl), (1 - xh, 1 - xl), (1 - xh, xl)]

    def gx_copy(n, arriving=False):
        if arriving:
            src_xh, src_xl = sources[n + 1]
        else:
            src_xh, src_xl = xh, xl
        return copy(g_ref, g_block(src_xh, y, src_xl, core), gx_s.at[n], gx_r.at[n], x_peers[n])

    for n in (2, 1, 0):
        gx_copy(n).start()

    def w_copy(j):
        rows = pl.ds((1 - xl) * half + j * HC, HC)
        return copy(w_ref.at[rows], wx.at[pl.ds(j * HC, HC)], w_s.at[j], w_r.at[j], across)

    @pl.loop(0, NJ)
    def _(j):
        w_copy(j).start()

    def source(b, y_):
        return sources[b][0], y_, sources[b][1]

    def gy_copy(b, d, arriving=False):
        y_ = ((y + NY - 1) if d == 0 else (y + 1)) % NY if arriving else y
        block = g_block(*source(b, y_), core)
        return copy(block, block, gy_s.at[d, b], gy_r.at[d, b], y_peers[d])

    def gf_copy(b, arriving=False):
        d = b % 2
        y_ = (y + 2) % NY if arriving else ((y + NY - 1) if d == 0 else (y + 1)) % NY
        block = g_block(*source(b, y_), core)
        return copy(block, block, gf_s.at[b], gf_r.at[b], y_peers[d])

    def gs_copy(b, n, arriving=False):
        block = g_block(*source(b, (y + NY - n) % NY), 1 - core if arriving else core)
        return copy(block, block, gs_s.at[n, b], gs_r.at[n, b], sibling)

    def along_y(b):
        for d in range(2):
            gy_copy(b, d).start()
        gs_copy(b, 0).start()

    def further(b):
        for d in range(2):
            gy_copy(b, d, True).wait_recv()
        gf_copy(b).start()
        gs_copy(b, 1).start()
        gs_copy(b, 3).start()

    g_load.wait()
    along_y(0)
    slot(0)
    slot(1)
    for n in (0, 1):
        gx_copy(n, True).wait_recv()
        along_y(n + 1)
    slot(2)
    gx_copy(2, True).wait_recv()
    along_y(3)
    slot(3)
    further(0)
    further(1)
    slot(4)
    further(2)
    further(3)
    slot(5)
    for b in range(4):
        gf_copy(b, True).wait_recv()
        gs_copy(b, 2).start()
    w_load.wait()
    for n in (0, 1, 3, 2):
        for b in range(4):
            gs_copy(b, n, True).wait_recv()
    slot(6)

    def rs_copy(d, s, j):
        if s == 0:
            return copy(h_snd.at[d, j], h_rcv.at[d, j], r_s.at[d, s, j], r_r.at[d, s, j], ring[d])
        return copy(f_snd.at[d, s - 1, j], f_rcv.at[d, s - 1, j], r_s.at[d, s, j], r_r.at[d, s, j], ring[d])

    def halves(j, owner):
        return [pbuf[j, pl.ds((k * NZ + owner) * TOK, TOK), :] for k in range(2)]

    def partial(j):
        w_copy(j).wait_recv()
        rows = pl.ds(j * HC, HC)
        nt = (((1,), (1,)), ((), ()))
        pbuf[j] = lax.dot_general(gbuf[xl], w_here[pl.ds(xl * half + j * HC, HC)], nt, preferred_element_type=F32) + lax.dot_general(
            gbuf[1 - xl], wx[rows], nt, preferred_element_type=F32
        )
        far = halves(j, (z + 4) % NZ)
        for d in range(2):
            encode([far[d]], h_snd.at[d, j], TOK)
            rs_copy(d, 0, j).start()

    def pass_on(s, j):
        for d in range(2):
            rs_copy(d, s - 1, j).wait_recv()
            owner = (z + 4 - s) % NZ if d == 0 else (z + 4 + s) % NZ
            parts = halves(j, owner)
            if s == 1:
                (arrived,) = decode(h_rcv.at[d, j], 1, TOK)
                parts[d] = parts[d] + arrived
            else:
                arrived = decode(f_rcv.at[d, s - 2, j], 2, TOK)
                parts = [p + q for p, q in zip(parts, arrived)]
            encode(parts, f_snd.at[d, s - 1, j], TOK)
            rs_copy(d, s, j).start()

    def i_copy(j):
        return copy(i_snd.at[j], i_rcv.at[j], i_s.at[j], i_r.at[j], across)

    def finish(j):
        parts = halves(j, z)
        for d in range(2):
            rs_copy(d, 3, j).wait_recv()
            parts = [p + q for p, q in zip(parts, decode(f_rcv.at[d, 2, j], 2, TOK))]
        mine, theirs = jnp.where(xl == 0, parts[0], parts[1]), jnp.where(xl == 0, parts[1], parts[0])
        ig_ref[:, pl.ds(pl.multiple_of(xl * half + j * HC, HC), HC)] = mine.astype(BF16)
        i_snd[j] = theirs.astype(BF16)
        i_copy(j).start()

    def x_copy(j):
        return copy(x_snd.at[j], x_rcv.at[j], x_s.at[j], x_r.at[j], across)

    def weight_part(j):
        for d in range(2):
            a_copy(d, 3, j, True).wait_recv()
        tn = (((0,), (0,)), ((), ()))
        tokens = pl.ds(xl * NZ * TOK, NZ * TOK)
        theirs = scaling * lax.dot_general(abuf[j], gbuf[1 - xl, tokens], tn, preferred_element_type=F32)
        encode([theirs[:, i * 128 : (i + 1) * 128] for i in range(4)], x_snd.at[j], FC)
        x_copy(j).start()
        wg_ref[pl.ds(j * FC, FC), :] = scaling * lax.dot_general(abuf[j], gbuf[xl, tokens], tn, preferred_element_type=F32)

    @pl.loop(0, NJ + 7)
    def _(i):
        def at(delay, work):
            @pl.when(jnp.logical_and(i >= delay, i < NJ + delay))
            def _():
                work(i - delay)

        at(0, partial)
        at(1, functools.partial(pass_on, 1))
        at(0, weight_part)
        for s in (1, 2, 3):

            @pl.when(i < s)
            def _():
                a_step(s, i + NJ - s)

        at(3, functools.partial(pass_on, 2))
        at(5, functools.partial(pass_on, 3))
        at(7, finish)

    @pl.loop(0, NJ)
    def _(j):
        i_copy(j).wait_recv()
        ig_ref[:, pl.ds(pl.multiple_of((1 - xl) * half + j * HC, HC), HC)] = i_rcv[j]
        x_copy(j).wait_recv()
        arrived = decode(x_rcv.at[j], 4, FC)
        for i in range(4):
            lanes = slice(i * 128, (i + 1) * 128)
            rows = pl.ds(j * FC, FC)
            wg_ref[rows, lanes] = wg_ref[rows, lanes] + arrived[i]

    @pl.loop(0, NJ)
    def _(j):
        w_copy(j).wait_send()
        x_copy(j).wait_send()
        i_copy(j).wait_send()
        for d in range(2):
            for s in range(4):
                a_copy(d, s, j).wait_send()
                rs_copy(d, s, j).wait_send()

    for n in range(3):
        gx_copy(n).wait_send()
    for b in range(4):
        for d in range(2):
            gy_copy(b, d).wait_send()
        gf_copy(b).wait_send()
        for n in range(4):
            gs_copy(b, n).wait_send()


def body(out_grad, acts, weight):
    dma = pltpu.SemaphoreType.DMA
    ff, features = weight.shape
    return pl.pallas_call(
        functools.partial(kernel, 1, 1.0 / math.sqrt(TOK * 16)),
        out_shape=(pltpu.VMEM(acts.shape, BF16), pltpu.VMEM(weight.shape, F32)),
        in_specs=[pl.BlockSpec(memory_space=pltpu.HBM)] * 3,
        out_specs=(pl.BlockSpec(memory_space=pltpu.VMEM), pl.BlockSpec(memory_space=pltpu.VMEM)),
        scratch_shapes=[
            pltpu.VMEM((2, 2 * NZ * TOK, features), BF16),
            pltpu.VMEM((ff // 2, features), BF16),
            pltpu.VMEM((ff, features), BF16),
            pltpu.VMEM((NJ, NZ * TOK, FC), BF16),
            pltpu.VMEM((NJ, 2 * NZ * TOK, HC), F32),
            pltpu.VMEM((2, NJ, TOK + 16, 128), BF16),
            pltpu.VMEM((2, NJ, TOK + 16, 128), BF16),
            pltpu.VMEM((2, 3, NJ, 2 * TOK + 16, 128), BF16),
            pltpu.VMEM((2, 3, NJ, 2 * TOK + 16, 128), BF16),
            pltpu.VMEM((NJ, 4 * FC + 16, 128), BF16),
            pltpu.VMEM((NJ, 4 * FC + 16, 128), BF16),
            pltpu.VMEM((NJ, TOK, HC), BF16),
            pltpu.VMEM((NJ, TOK, HC), BF16),
            dma((3,)), dma((3,)),
            dma((2, 4)), dma((2, 4)),
            dma((4,)), dma((4,)),
            dma((4, 4)), dma((4, 4)),
            dma((NJ,)), dma((NJ,)),
            dma((2, 4, NJ)), dma((2, 4, NJ)),
            dma((2, 4, NJ)), dma((2, 4, NJ)),
            dma((NJ,)), dma((NJ,)),
            dma((NJ,)), dma((NJ,)),
            dma((NJ + 2,)),
        ],
        compiler_params=pltpu.CompilerParams(
            collective_id=0, has_side_effects=True, vmem_limit_bytes=56 * 2**20
        ),
        cost_estimate=pl.CostEstimate(
            flops=8 * NZ * TOK * ff * features, bytes_accessed=16 * 2**20, transcendentals=6 * 2**20
        ),
    )(out_grad, acts, weight)


def solution(mesh):
    in_specs = (P("row", "col"), P("col", "row"), P("row", "col"))
    out_specs = (P("col", "row"), P("row", "col"))
    return jax.shard_map(body, mesh=mesh, in_specs=in_specs, out_specs=out_specs, check_vma=False)
```

time: 96.9 us -> 95.4 us (0.985); the launches traced: 96.8 us -> 94.2 us
  Pallas kernels: 93.6 us -> 91 us
    pallas_call x1, Pallas kernels: 93.6 us -> 91 us  [body(): pl.pallas_call(functools.partial(kernel, 1, 1.0 / math.sqrt(TOK * 16)), o...]
where the time goes in v3:
time: 95.4 us; the launch traced here: 94.2 us
  Pallas kernels  91 us (95%)
  local copies, waits for them, and re-layouts  2.61 us (3%)
    pallas_call x1, Pallas kernels, body(): pl.pallas_call(functools.partial(kernel, 1, 1.0 / math.sqrt(TOK * 16)), o...  91 us
    unnamed x2, local copies, waits for them, and re-layouts  2.61 us

profile of v3, /device:TPU:8, one launch (start us, length us, event | category | flops | bytes accessed | tf_op | source)
XLA Modules:
  0.0 94.2 jit_solution(2447385763443890644)
XLA Ops:
  0.6 91.0 %shard_map.50 = (bf16[128,1792]{1,0:T(8,128)(2,1)S(1)}, f32[1792,512]{1,0:T(8,128)S(1)}) custom-call(bf16[128,512]{1,0:T(8,128)(2,1)} %g_ref.1, bf16[128,1792]{1,0:T(8,128)(2,1)} %a_ref.1, bf16[1792,512]{1,0:T(8,128)(2,1)} %w_ref.1), custom_call_target="tpu_custom_call" | custom-call | flops 7516192768 | bytes 16777216 | tf_op jit(solution)/shard_map/pallas_call | solution.py:297
  91.6 0.8 copy.7
  92.4 1.8 %copy.8 = f32[1792,512]{1,0:T(8,128)} copy(f32[1792,512]{1,0:T(8,128)S(1)} %get-tuple-element.3) | data formatting | bytes 7340032
